TPU v7x, 512 devices: a whole 4x8x8 slice. The times are simulated.
512 devices in a mesh: row: 32 (over y, x), col: 16 (over z, core).
Axes of the slice: x: 4, y: 8, z: 8, core: 2. Of those that a mesh axis runs over, the one named last changes fastest.
Arguments:
- tokens: bfloat16 [256, 8192], P('row', 'col'), may hold values from -6 to 6
- w_gate: bfloat16 [8192, 24576], P('col', 'row'), may hold values from -0.0625 to 0.0625
- w_up: bfloat16 [8192, 24576], P('col', 'row'), may hold values from -0.0625 to 0.0625
- w_down: bfloat16 [24576, 8192], P('row', 'col'), may hold values from -0.0390625 to 0.0390625
- target_table: bfloat16 [128, 8192], P(None, 'col'), may hold values from -6 to 6
- target_rows: int32 [128], P('row'), may hold values from 0 to 255, as said below
- buckets: int32 [128], P('row'), may hold values from 0 to 127
Outputs:
- output_y: bfloat16 [256, 8192], P('row', 'col')
- grad_tokens: bfloat16 [256, 8192], P('row', 'col')
- grad_gate: bfloat16 [8192, 24576], P('col', 'row')
- grad_up: bfloat16 [8192, 24576], P('col', 'row')
- grad_down: bfloat16 [24576, 8192], P('row', 'col')
Inputs may be any that keep to these rules, and one draw needn't show every extreme that they name: `target_rows`: entries k * 4 to (k + 1) * 4 - 1 name distinct rows among rows k * 8 to (k + 1) * 8 - 1.
All inputs are finite; a program needn't handle non-finite values.
Results may differ from a plain program's by a relative error of at most 0.008.
Values may be sent and summed in bfloat16 or wider, within the bound.
A program may use at most 64 MiB of HBM per device.

v0:
```python
import jax
import jax.numpy as jnp
from jax import lax
from jax.sharding import PartitionSpec as P


def act_grads(grad_hidden, gate, up):
    sig = jax.nn.sigmoid(gate)
    gate_act = (grad_hidden * up * sig * (1.0 + gate * (1.0 - sig))).astype(jnp.bfloat16)
    up_act = (grad_hidden * gate * sig).astype(jnp.bfloat16)
    return (gate_act, up_act)


def lhs_product(left, right):
    return lax.dot_general(
        left, right, (((0,), (0,)), ((), ())), preferred_element_type=jnp.float32
    )


def rhs_product(left, right):
    return lax.dot_general(
        left, right, (((1,), (1,)), ((), ())), preferred_element_type=jnp.float32
    )


def on_device(tokens, w_gate, w_up, w_down, target_table, target_rows, buckets):
    own_rows = tokens.shape[0]
    hid_width = w_gate.shape[1]
    x_full = lax.all_gather(tokens, "row", axis=0, tiled=True)
    both_sums = lax.psum_scatter(
        jnp.concatenate(
            [
                jnp.dot(x_full, w_gate, preferred_element_type=jnp.float32),
                jnp.dot(x_full, w_up, preferred_element_type=jnp.float32),
            ],
            axis=1,
        ),
        "col",
        scatter_dimension=0,
        tiled=True,
    )
    gate = both_sums[:, :hid_width]
    up = both_sums[:, hid_width:]
    sig = jax.nn.sigmoid(gate)
    hidden_rows = (gate * sig * up).astype(jnp.bfloat16)
    hidden = lax.all_gather(hidden_rows, "col", axis=0, tiled=True)
    output_y = lax.psum_scatter(
        jnp.dot(hidden, w_down, preferred_element_type=jnp.float32),
        "row",
        scatter_dimension=0,
        tiled=True,
    ).astype(jnp.bfloat16)
    local_rows = target_rows - lax.axis_index("row") * own_rows
    onehot = (
        buckets[:, None] == jnp.arange(target_table.shape[0], dtype=jnp.int32)[None, :]
    ).astype(jnp.bfloat16)
    targets = jnp.dot(onehot, target_table, preferred_element_type=jnp.float32)
    diff = 0.25 * (output_y[local_rows].astype(jnp.float32) - targets)
    grad_y = jnp.zeros(output_y.shape, jnp.float32).at[local_rows].set(diff).astype(jnp.bfloat16)
    grad_full = lax.all_gather(grad_y, "row", axis=0, tiled=True)
    grad_down = lhs_product(hidden, grad_full).astype(jnp.bfloat16)
    grad_hidden = lax.psum_scatter(
        rhs_product(grad_full, w_down), "col", scatter_dimension=0, tiled=True
    )
    gate_rows, up_rows = act_grads(grad_hidden, gate, up)
    gate_act, up_act = (
        lax.all_gather(gate_rows, "col", axis=0, tiled=True),
        lax.all_gather(up_rows, "col", axis=0, tiled=True),
    )
    grad_gate = lhs_product(x_full, gate_act).astype(jnp.bfloat16)
    grad_up = lhs_product(x_full, up_act).astype(jnp.bfloat16)
    grad_tokens = lax.psum_scatter(
        rhs_product(gate_act, w_gate) + rhs_product(up_act, w_up),
        "row",
        scatter_dimension=0,
        tiled=True,
    ).astype(jnp.bfloat16)
    return (output_y, grad_tokens, grad_gate, grad_up, grad_down)


def solution(mesh):
    in_specs = (
        P("row", "col"),
        P("col", "row"),
        P("col", "row"),
        P("row", "col"),
        P(None, "col"),
        P("row"),
        P("row"),
    )
    out_specs = (
        P("row", "col"),
        P("row", "col"),
        P("col", "row"),
        P("col", "row"),
        P("row", "col"),
    )
    return jax.shard_map(
        on_device, mesh=mesh, in_specs=in_specs, out_specs=out_specs, check_vma=False
    )
```

profile of v0, /device:TPU:1, one launch (start us, length us, event | category | flops | bytes accessed | tf_op | source)
XLA Modules:
  0.0 724.4 jit_solution(1459906840517392470)
XLA Ops:
  7.2 0.0 copy-start
  7.2 0.0 copy-start.1
  7.2 0.0 reduce-scatter.5.cloned.1.call-start
  7.2 38.8 %all_gather.15 = bf16[256,512]{1,0:T(8,128)(2,1)S(1)} all-gather(bf16[8,512]{1,0:T(8,128)(2,1)} %param.7), channel_id=1, replica_groups=mesh['row'=32,'col'=16] {'row'}, dimensions={0}, use_global_device_ids=true | all-gather | bytes 270336 | tf_op jit(solution)/shard_map/all_gather | solution.py:29
  46.1 1.5 fusion.6
  47.6 0.0 copy-done.1
  47.6 0.4 fusion.7
  48.0 1.3 pad_maximum_fusion
  49.3 0.0 reduce-scatter.5.cloned.1.call-update
  49.3 0.0 copy-start.8
  49.3 0.0 copy-start.7
  49.3 0.0 copy-start.9
  49.4 0.0 reduce-scatter.7.cloned.1.call-start
  49.4 72.6 %reduce-scatter.5.cloned.1.call-done = f32[16,1536]{1,0:T(8,128)} async-done(((f32[256,1536]{1,0:T(8,128)}), f32[16,1536]{1,0:T(8,128)}) %reduce-scatter.5.cloned.1.call-update) | async-done | bytes 98320 | tf_op jit(solution)/shard_map/reduce_scatter | solution.py:30
  122.0 0.8 multiply_convert_fusion.2
  122.9 18.7 %all_gather.16 = bf16[256,768]{1,0:T(8,128)(2,1)S(1)} all-gather(bf16[16,768]{1,0:T(8,128)(2,1)S(1)} %multiply_convert_fusion.2), channel_id=1, replica_groups=mesh['row'=32,'col'=16] {'col'}, dimensions={0}, use_global_device_ids=true | all-gather | bytes 417792 | tf_op jit(solution)/shard_map/all_gather | solution.py:46
  141.6 0.0 copy-done
  141.6 1.2 fusion.8
  142.7 0.0 reduce-scatter.7.cloned.1.call-update
  142.8 0.0 reduce-scatter.9.cloned.1.call-start
  142.8 0.0 copy-done.8
  142.9 211.1 %reduce-scatter.7.cloned.1.call-done = f32[8,512]{1,0:T(8,128)} async-done(((f32[256,512]{1,0:T(8,128)}), f32[8,512]{1,0:T(8,128)}) %reduce-scatter.7.cloned.1.call-update) | async-done | bytes 16400 | tf_op jit(solution)/shard_map/reduce_scatter | solution.py:47
  353.9 0.7 convert_element_type.38
  354.7 0.6 gather_fusion
  355.2 0.2 fusion.2
  355.4 0.6 scatter_custom_fusion
  356.1 35.3 %all_gather.17 = bf16[256,512]{1,0:T(8,128)(2,1)S(1)} all-gather(bf16[8,512]{1,0:T(8,128)(2,1)S(1)} %convert_element_type.40), channel_id=1, replica_groups=mesh['row'=32,'col'=16] {'row'}, dimensions={0}, use_global_device_ids=true | all-gather | bytes 270336 | tf_op jit(solution)/shard_map/all_gather | solution.py:60
  391.4 0.7 copy-done.3
  392.1 1.3 fusion.9
  393.4 0.0 reduce-scatter.9.cloned.1.call-update
  393.4 0.0 reduce-scatter.11.cloned.1.call-start
  393.4 74.1 %reduce-scatter.9.cloned.1.call-done = f32[16,768]{1,0:T(8,128)} async-done(((f32[256,768]{1,0:T(8,128)}), f32[16,768]{1,0:T(8,128)}) %reduce-scatter.9.cloned.1.call-update) | async-done | bytes 49168 | tf_op jit(solution)/shard_map/reduce_scatter | solution.py:62
  467.5 0.0 copy-done.5
  467.5 0.8 multiply_convert_fusion
  468.4 18.6 %all_gather.18 = bf16[256,768]{1,0:T(8,128)(2,1)S(1)} all-gather(bf16[16,768]{1,0:T(8,128)(2,1)S(1)} %get-tuple-element.11), channel_id=1, replica_groups=mesh['row'=32,'col'=16] {'col'}, dimensions={0}, use_global_device_ids=true | all-gather | bytes 417792 | tf_op jit(solution)/shard_map/all_gather | solution.py:67
  487.0 0.4 fusion.10
  487.4 0.0 copy-start.4
  487.4 17.3 %all_gather.19 = bf16[256,768]{1,0:T(8,128)(2,1)S(1)} all-gather(bf16[16,768]{1,0:T(8,128)(2,1)S(1)} %get-tuple-element.10), channel_id=1, replica_groups=mesh['row'=32,'col'=16] {'col'}, dimensions={0}, use_global_device_ids=true | all-gather | bytes 417792 | tf_op jit(solution)/shard_map/all_gather | solution.py:68
  504.6 1.2 convolution_add_fusion
  505.8 0.0 reduce-scatter.11.cloned.1.call-update
  505.9 0.0 copy-done.4
  505.9 1.3 convolution_convert_fusion
  507.2 0.4 fusion
  507.6 1.2 copy.12
  508.7 0.4 fusion.1
  509.1 1.2 copy.13
  510.3 206.3 %reduce-scatter.11.cloned.1.call-done = f32[8,512]{1,0:T(8,128)} async-done(((f32[256,512]{1,0:T(8,128)}), f32[8,512]{1,0:T(8,128)}) %reduce-scatter.11.cloned.1.call-update) | async-done | bytes 16400 | tf_op jit(solution)/shard_map/reduce_scatter | solution.py:72
  716.6 1.3 convert_element_type.43
  (11 shorter events, 0.0 us)
Async XLA Ops:
  7.2 134.4 %copy-start = (bf16[768,512]{1,0:T(8,128)(2,1)S(1)}, bf16[768,512]{1,0:T(8,128)(2,1)}, u32[]{:S(2)}) copy-start(bf16[768,512]{1,0:T(8,128)(2,1)} %param.10) | copy-start | bytes 2359300
  7.2 40.4 %copy-start.1 = (bf16[512,768]{1,0:T(8,128)(2,1)S(1)}, bf16[512,768]{1,0:T(8,128)(2,1)}, u32[]{:S(2)}) copy-start(bf16[512,768]{1,0:T(8,128)(2,1)} %param.9) | copy-start | bytes 2359300
  7.2 114.8 %reduce-scatter.5.cloned.1.call-start = ((), (), s32[]{:S(2)}) async-start(), calls=%async_computation.4 | async-start | bytes 1671168 | tf_op jit(solution)/shard_map/reduce_scatter | solution.py:30
  49.3 93.5 %copy-start.8 = (s32[4]{0:T(128)S(1)}, s32[4]{0:T(128)}, u32[]{:S(2)}) copy-start(s32[4]{0:T(128)} %param.12) | copy-start | bytes 52
  49.3 305.9 %copy-start.7 = (bf16[128,512]{1,0:T(8,128)(2,1)S(1)}, bf16[128,512]{1,0:T(8,128)(2,1)}, u32[]{:S(2)}) copy-start(bf16[128,512]{1,0:T(8,128)(2,1)} %param.11) | copy-start | bytes 393220
  49.3 305.9 %copy-start.9 = (s32[4]{0:T(128)S(1)}, s32[4]{0:T(128)}, u32[]{:S(2)}) copy-start(s32[4]{0:T(128)} %param.13) | copy-start | bytes 52
  49.4 304.6 %reduce-scatter.7.cloned.1.call-start = ((), (), s32[]{:S(2)}) async-start(), calls=%async_computation.5 | async-start | bytes 540672 | tf_op jit(solution)/shard_map/reduce_scatter | solution.py:47
  142.8 324.7 %reduce-scatter.9.cloned.1.call-start = ((), (), s32[]{:S(2)}) async-start(), calls=%async_computation.6 | async-start | bytes 835584 | tf_op jit(solution)/shard_map/reduce_scatter | solution.py:62
  354.7 113.7 %copy-start.6 = (bf16[8,512]{1,0:T(8,128)(2,1)}, bf16[8,512]{1,0:T(8,128)(2,1)S(1)}, u32[]{:S(2)}) copy-start(bf16[8,512]{1,0:T(8,128)(2,1)S(1)} %convert_element_type.38) | copy-start | bytes 24580
  354.7 112.9 %copy-start.5 = (f32[16,1536]{1,0:T(8,128)S(1)}, f32[16,1536]{1,0:T(8,128)}, u32[]{:S(2)}) copy-start(f32[16,1536]{1,0:T(8,128)} %reduce-scatter.5.cloned.1.call-done) | copy-start | bytes 294916
  391.4 0.7 copy-start.3
  392.1 94.9 %copy-start.2 = (bf16[512,768]{1,0:T(8,128)(2,1)S(1)}, bf16[512,768]{1,0:T(8,128)(2,1)}, u32[]{:S(2)}) copy-start(bf16[512,768]{1,0:T(8,128)(2,1)} %param.8) | copy-start | bytes 2359300
  393.4 323.2 %reduce-scatter.11.cloned.1.call-start = ((), (), s32[]{:S(2)}) async-start(), calls=%async_computation.7 | async-start | bytes 540672 | tf_op jit(solution)/shard_map/reduce_scatter | solution.py:72
  487.4 18.5 %copy-start.4 = (bf16[256,512]{1,0:T(8,128)(2,1)S(1)}, bf16[256,512]{1,0:T(8,128)(2,1)}, u32[]{:S(2)}) copy-start(bf16[256,512]{1,0:T(8,128)(2,1)} %copy-done.3) | copy-start | bytes 786436
Sparse Core Ops, SparseCore 0:
  49.4 72.5 reduce-scatter.4
  142.9 211.0 reduce-scatter.6
  393.5 73.9 reduce-scatter.8
  506.0 210.5 reduce-scatter.10
where the time goes:
time: 729 us; the launch traced here: 724 us
  waiting for transfers between devices  564 us (77%)
  blocking collectives  129 us (18%)
  between operations  13.9 us (2%)
  matrix products  8.15 us (1%)
    reduce_scatter x1, waiting for transfers between devices, on_device(): lax.psum_scatter(jnp.dot(hidden, w_down, preferred_element_type=jnp.float...  211 us
    reduce_scatter x1, waiting for transfers between devices, on_device(): lax.psum_scatter(rhs_product(gate_act, w_gate) + rhs_product(up_act, w_up...  206 us
    reduce_scatter x1, waiting for transfers between devices, on_device(): lax.psum_scatter(rhs_product(grad_full, w_down), 'col', scatter_dimension...  74.1 us
    reduce_scatter x1, waiting for transfers between devices, on_device(): lax.psum_scatter(jnp.concatenate([jnp.dot(x_full, w_gate, preferred_eleme...  72.6 us
    all_gather x1, blocking collectives, on_device(): x_full = lax.all_gather(tokens, 'row', axis=0, tiled=True)  38.8 us
    all_gather x1, blocking collectives, on_device(): grad_full = lax.all_gather(grad_y, 'row', axis=0, tiled=True)  35.3 us
    all_gather x1, blocking collectives, on_device(): hidden = lax.all_gather(hidden_rows, 'col', axis=0, tiled=True)  18.7 us
    all_gather x1, blocking collectives, on_device(): lax.all_gather(gate_rows, 'col', axis=0, tiled=True)  18.6 us
  transfers between devices with their start and end apart: 4, of which 4 were waited for; matrix products, arithmetic and copies ran while one was open for 1% of the time, Pallas kernels for 0%

commit v1 on v0

v1 whole, which is shorter than its diff:
```python
import jax
import jax.numpy as jnp
from jax import lax
from jax.experimental import pallas as pl
from jax.experimental.pallas import tpu as pltpu
from jax.sharding import PartitionSpec as P

MESH = pl.DeviceIdType.MESH
BF16, F32 = jnp.bfloat16, jnp.float32

NY, NX, NZ = 8, 4, 8
ROWS = NY * NX
HALF = 4
LANES = 128
TOK = ROWS * HALF

(
    S_A0, S_A1, S_BP0, S_BP1, S_B0, S_B1, S_C0, S_C1, S_CP0, S_CP1, S_D0, S_D1,
    S_E, S_FP, S_F, S_G, S_GP, S_H, NUM_SEMS,
) = range(19)


def zigzag(m, n):
    half = (m + 1) // 2
    return n // 2 + jnp.where(m % 2 == 0, half, -half)


def dot(left, right, dims):
    return lax.dot_general(left, right, ((dims[0], dims[1]), ((), ())), preferred_element_type=F32)


def kernel(
    rows_s, buckets_s, tokens_ref, wg_hbm, wu_hbm, wd_hbm, table_hbm,
    y_out, gt_out, gg_out, gu_out, gd_out,
    wg, wu, wd, table,
    xs, xr, f_in, x_mat,
    gu_part, gu_psend, gu_precv, gu_zsend, gu_zrecv, gu_keep,
    hc, h_mat,
    f_out, y_send, y_recv, y_keep, tgt,
    gy_send, gy_recv, gy_mat,
    gh_part, gh_psend, gh_precv, gh_zsend, gh_zrecv,
    ac, act_mat, gt_send, gt_recv,
    send_sem, recv_sem, load_sem,
):
    row, col = lax.axis_index("row"), lax.axis_index("col")
    y, x, z, k = row // NX, row % NX, col // 2, col % 2
    width = wg.shape[1]
    wide = wg.shape[0]
    chunks = wide // LANES
    half_width = width // 2

    loads = [
        pltpu.make_async_copy(src, dst, load_sem.at[i])
        for i, (src, dst) in enumerate([(wg_hbm, wg), (wu_hbm, wu), (wd_hbm, wd), (table_hbm, table)])
    ]
    for load in loads:
        load.start()

    def row_peer(m, sign):
        dy, dx = zigzag(m // NX, NY), zigzag(m % NX, NX)
        return (((y + NY + sign * dy) % NY) * NX + (x + NX + sign * dx) % NX, col)

    def z_peer(m):
        return (z + zigzag(m, NZ)) % NZ

    partner = (row, z * 2 + 1 - k)

    barrier = pltpu.get_barrier_semaphore()

    def greet_row(m, carry):
        pl.semaphore_signal(barrier, inc=1, device_id=row_peer(m, 1), device_id_type=MESH)
        return carry

    def greet_col(m, carry):
        pl.semaphore_signal(barrier, inc=1, device_id=(row, z_peer(m) * 2 + k), device_id_type=MESH)
        return carry

    lax.fori_loop(0, ROWS - 1, greet_row, 0)
    lax.fori_loop(0, NZ - 1, greet_col, 0)
    pl.semaphore_signal(barrier, inc=1, device_id=partner, device_id_type=MESH)

    tgt_pos = [rows_s[i] - 2 * HALF * row for i in range(HALF)]
    rest_pos = [jnp.int32(0)] * HALF
    seen = jnp.int32(0)
    for t in range(2 * HALF):
        is_target = jnp.int32(0)
        for p in tgt_pos:
            is_target = is_target + jnp.where(p == t, 1, 0)
        for i in range(HALF):
            rest_pos[i] = rest_pos[i] + jnp.where(seen == i, 1 - is_target, 0) * t
        seen = seen + 1 - is_target
    pos = [tgt_pos, rest_pos]

    tok = tokens_ref[...].astype(F32)
    iota8 = lax.broadcasted_iota(jnp.int32, tok.shape, 0)
    iota16 = lax.broadcasted_iota(jnp.int32, (16, LANES), 0)
    for h in range(2):
        packed = jnp.zeros((16, LANES), F32)
        for i in range(HALF):
            line = jnp.sum(jnp.where(iota8 == pos[h][i], tok, 0.0), axis=0, keepdims=True)
            for j in range(chunks):
                piece = line[:, j * LANES : (j + 1) * LANES]
                packed = jnp.where(iota16 == j * HALF + i, piece, packed)
        xs[h] = packed.astype(BF16)
        xr[h, ROWS - 1] = packed.astype(BF16)

    loads[3].wait()
    targets = jnp.zeros((16, LANES), F32)
    lane16 = lax.broadcasted_iota(jnp.int32, (16, table.shape[0]), 1)
    sub16 = lax.broadcasted_iota(jnp.int32, (16, table.shape[0]), 0)
    for j in range(chunks):
        onehot = jnp.zeros((16, table.shape[0]), F32)
        for i in range(HALF):
            hit = jnp.logical_and(sub16 == j * HALF + i, lane16 == buckets_s[i])
            onehot = jnp.where(hit, 1.0, onehot)
        targets = targets + dot(onehot.astype(BF16), table[:, j * LANES : (j + 1) * LANES], ((1,), (0,)))
    tgt[...] = targets

    pl.semaphore_wait(barrier, ROWS - 1 + NZ - 1 + 1)

    def wait_recv(ref, s):
        pltpu.make_async_copy(ref, ref, recv_sem.at[s]).wait()

    def wait_send(ref, s):
        pltpu.make_async_copy(ref, ref, send_sem.at[s]).wait()

    def remote(src, dst, s, device):
        pltpu.make_async_remote_copy(
            src_ref=src, dst_ref=dst, send_sem=send_sem.at[s], recv_sem=recv_sem.at[s],
            device_id=device, device_id_type=MESH,
        ).start()

    def spread_rows(src, dst, s):
        def one(m, carry):
            remote(src, dst.at[m], s, row_peer(m, 1))
            return carry

        lax.fori_loop(0, ROWS - 1, one, 0)

    def scatter_rows(src, dst, s):
        def one(m, carry):
            remote(src.at[m], dst.at[m], s, row_peer(m, -1))
            return carry

        lax.fori_loop(0, ROWS - 1, one, 0)

    def scatter_z(src, dst, s):
        def one(m, carry):
            peer = z_peer(m)
            remote(src.at[peer], dst.at[z], s, (row, peer * 2 + k))
            return carry

        lax.fori_loop(0, NZ - 1, one, 0)

    def spread_z(buf, s):
        def one(m, carry):
            remote(buf.at[k, z], buf.at[k, z], s, (row, z_peer(m) * 2 + k))
            return carry

        lax.fori_loop(0, NZ - 1, one, 0)

    def others(buf, n):
        return buf.at[pl.ds(0, n - 1)]

    def to_matrix(buf, out):
        f_in[...] = buf[...].astype(F32).reshape(ROWS * 16, LANES)
        for j in range(chunks):
            parts = [f_in[pl.ds(j * HALF + i, ROWS, stride=16), :] for i in range(HALF)]
            out[:, j * LANES : (j + 1) * LANES] = jnp.concatenate(parts, axis=0).astype(BF16)

    def from_matrix(mat, out):
        for j in range(chunks):
            for i in range(HALF):
                f_out[pl.ds(j * HALF + i, ROWS, stride=16), :] = mat[
                    i * ROWS : (i + 1) * ROWS, j * LANES : (j + 1) * LANES
                ]
        out[...] = f_out[...].reshape(ROWS, 16, LANES).astype(BF16)

    def row_total(recv):
        own = f_out[(ROWS - 1) * 16 : ROWS * 16, :]
        return own + jnp.sum(recv[...].astype(F32), axis=0)

    def unpack(first, second, out):
        iota = lax.broadcasted_iota(jnp.int32, (2 * HALF, LANES), 0)
        for j in range(chunks):
            block = jnp.zeros((2 * HALF, LANES), F32)
            for h, v in enumerate((first, second)):
                for i in range(HALF):
                    at = j * HALF + i
                    block = jnp.where(iota == pos[h][i], v[at : at + 1, :], block)
            out[:, j * LANES : (j + 1) * LANES] = block.astype(BF16)

    def gate_up_part(h):
        to_matrix(xr.at[h], x_mat.at[h])
        xm = x_mat[h]
        gate = dot(xm, wg[...], ((1,), (0,)))
        gu_part[:, :, 0:8, :] = gate.reshape(2, NZ, 8, width)
        up = dot(xm, wu[...], ((1,), (0,)))
        gu_part[:, :, 8:16, :] = up.reshape(2, NZ, 8, width)
        gu_psend[h] = gu_part[1 - k].astype(BF16)
        remote(gu_psend.at[h], gu_precv.at[h], S_BP0 + h, partner)

    def gate_up_scatter(h):
        wait_recv(gu_precv.at[h], S_BP0 + h)
        gu_zsend[h] = (gu_part[k] + gu_precv[h].astype(F32)).astype(BF16)
        gu_zrecv[h, z] = gu_zsend[h, z]
        scatter_z(gu_zsend.at[h], gu_zrecv.at[h], S_B0 + h)

    def hidden_spread(h):
        wait_recv(others(gu_zrecv.at[h], NZ), S_B0 + h)
        both = jnp.sum(gu_zrecv[h].astype(F32), axis=0)
        if h == 0:
            gu_keep[...] = both
        gate, up = both[0:8], both[8:16]
        hid = gate * jax.nn.sigmoid(gate) * up
        hc[h, k, z] = jnp.concatenate([hid[:, :half_width], hid[:, half_width:]], axis=0).astype(BF16)
        spread_z(hc.at[h], S_C0 + h)

    def hidden_pair(h):
        wait_recv(others(hc.at[h, 0], NZ), S_C0 + h)
        remote(hc.at[h, k], hc.at[h, k], S_CP0 + h, partner)

    def output_scatter(h):
        wait_recv(hc.at[h, 0], S_CP0 + h)
        v = hc[h].astype(F32).reshape(2 * NZ, 16, half_width)
        h_mat[h, :, :half_width] = v[:, 0:8].reshape(TOK, half_width).astype(BF16)
        h_mat[h, :, half_width:] = v[:, 8:16].reshape(TOK, half_width).astype(BF16)
        from_matrix(dot(h_mat[h], wd[...], ((1,), (0,))), y_send.at[h])
        y_keep[h] = f_out[(ROWS - 1) * 16 : ROWS * 16, :]
        scatter_rows(y_send.at[h], y_recv.at[h], S_D0 + h)

    def output_total(h):
        wait_recv(y_recv.at[h], S_D0 + h)
        total = y_keep[h] + jnp.sum(y_recv[h].astype(F32), axis=0)
        y_keep[h] = total.astype(BF16).astype(F32)

    spread_rows(xs.at[0], xr.at[0], S_A0)
    loads[0].wait()
    loads[1].wait()
    loads[2].wait()
    wait_recv(others(xr.at[0], ROWS), S_A0)
    gate_up_part(0)
    gate_up_scatter(0)
    spread_rows(xs.at[1], xr.at[1], S_A1)
    hidden_spread(0)
    wait_recv(others(xr.at[1], ROWS), S_A1)
    gate_up_part(1)
    hidden_pair(0)
    output_scatter(0)
    gate_up_scatter(1)
    output_total(0)

    gy = (0.25 * (y_keep[0] - tgt[...])).astype(BF16)
    gy_send[...] = gy
    gy_recv[ROWS - 1] = gy
    spread_rows(gy_send, gy_recv, S_E)
    hidden_spread(1)
    wait_recv(others(gy_recv, ROWS), S_E)

    to_matrix(gy_recv, gy_mat)
    gh = dot(gy_mat[...], wd[...], ((1,), (1,))).reshape(2, NZ, 8, width)
    gh_part[:, :, 0:8, :] = gh[:, :, :, :half_width]
    gh_part[:, :, 8:16, :] = gh[:, :, :, half_width:]
    gh_psend[...] = gh_part[1 - k].astype(BF16)
    remote(gh_psend, gh_precv, S_FP, partner)
    wait_recv(gh_precv, S_FP)
    gh_zsend[...] = (gh_part[k] + gh_precv[...].astype(F32)).astype(BF16)
    gh_zrecv[z] = gh_zsend[z]
    scatter_z(gh_zsend, gh_zrecv, S_F)
    hidden_pair(1)
    output_scatter(1)
    wait_recv(others(gh_zrecv, NZ), S_F)
    total = jnp.sum(gh_zrecv[...].astype(F32), axis=0)
    grad_hidden = jnp.concatenate([total[0:8], total[8:16]], axis=1)
    gate, up = gu_keep[0:8], gu_keep[8:16]
    sig = jax.nn.sigmoid(gate)
    gate_act = grad_hidden * up * sig * (1.0 + gate * (1.0 - sig))
    up_act = grad_hidden * gate * sig
    ac[k, z] = jnp.concatenate([gate_act, up_act], axis=0).astype(BF16)
    spread_z(ac, S_G)
    gd_out[...] = dot(h_mat[0], gy_mat[...], ((0,), (0,))).astype(BF16)
    wait_recv(others(ac.at[0], NZ), S_G)
    remote(ac.at[k], ac.at[k], S_GP, partner)
    wait_recv(ac.at[0], S_GP)
    v = ac[...].astype(F32).reshape(2 * NZ, 16, width)
    act_mat[0] = v[:, 0:8].reshape(TOK, width).astype(BF16)
    act_mat[1] = v[:, 8:16].reshape(TOK, width).astype(BF16)
    grad = dot(act_mat[0], wg[...], ((1,), (1,))) + dot(act_mat[1], wu[...], ((1,), (1,)))
    from_matrix(grad, gt_send)
    scatter_rows(gt_send, gt_recv, S_H)
    output_total(1)
    unpack(y_keep[0], y_keep[1], y_out)
    gg_out[...] = dot(x_mat[0], act_mat[0], ((0,), (0,))).astype(BF16)
    gu_out[...] = dot(x_mat[0], act_mat[1], ((0,), (0,))).astype(BF16)
    wait_recv(gt_recv, S_H)
    unpack(row_total(gt_recv), jnp.zeros((16, LANES), F32), gt_out)

    for h in range(2):
        wait_send(others(xr.at[h], ROWS), S_A0 + h)
        wait_send(gu_precv.at[h], S_BP0 + h)
        wait_send(others(gu_zrecv.at[h], NZ), S_B0 + h)
        wait_send(others(hc.at[h, 0], NZ), S_C0 + h)
        wait_send(hc.at[h, 0], S_CP0 + h)
        wait_send(y_recv.at[h], S_D0 + h)
    wait_send(others(gy_recv, ROWS), S_E)
    wait_send(gh_precv, S_FP)
    wait_send(others(gh_zrecv, NZ), S_F)
    wait_send(others(ac.at[0], NZ), S_G)
    wait_send(ac.at[0], S_GP)
    wait_send(gt_recv, S_H)


def on_device(tokens, w_gate, w_up, w_down, target_table, target_rows, buckets):
    wide, width = w_gate.shape
    half_width = width // 2
    vmem, smem, anywhere = (pl.BlockSpec(memory_space=s) for s in (pltpu.VMEM, pltpu.SMEM, pl.ANY))
    outs = (tokens, tokens, w_gate, w_up, w_down)
    return pl.pallas_call(
        kernel,
        out_shape=tuple(jax.ShapeDtypeStruct(a.shape, BF16) for a in outs),
        in_specs=[smem, smem, vmem, anywhere, anywhere, anywhere, anywhere],
        out_specs=(vmem,) * 5,
        scratch_shapes=[
            pltpu.VMEM(w_gate.shape, BF16),
            pltpu.VMEM(w_up.shape, BF16),
            pltpu.VMEM(w_down.shape, BF16),
            pltpu.VMEM(target_table.shape, BF16),
            pltpu.VMEM((2, 16, LANES), BF16),
            pltpu.VMEM((2, ROWS, 16, LANES), BF16),
            pltpu.VMEM((ROWS * 16, LANES), F32),
            pltpu.VMEM((2, TOK, wide), BF16),
            pltpu.VMEM((2, NZ, 16, width), F32),
            pltpu.VMEM((2, NZ, 16, width), BF16),
            pltpu.VMEM((2, NZ, 16, width), BF16),
            pltpu.VMEM((2, NZ, 16, width), BF16),
            pltpu.VMEM((2, NZ, 16, width), BF16),
            pltpu.VMEM((16, width), F32),
            pltpu.VMEM((2, 2, NZ, 16, half_width), BF16),
            pltpu.VMEM((2, TOK, width), BF16),
            pltpu.VMEM((ROWS * 16, LANES), F32),
            pltpu.VMEM((2, ROWS, 16, LANES), BF16),
            pltpu.VMEM((2, ROWS - 1, 16, LANES), BF16),
            pltpu.VMEM((2, 16, LANES), F32),
            pltpu.VMEM((16, LANES), F32),
            pltpu.VMEM((16, LANES), BF16),
            pltpu.VMEM((ROWS, 16, LANES), BF16),
            pltpu.VMEM((TOK, wide), BF16),
            pltpu.VMEM((2, NZ, 16, half_width), F32),
            pltpu.VMEM((NZ, 16, half_width), BF16),
            pltpu.VMEM((NZ, 16, half_width), BF16),
            pltpu.VMEM((NZ, 16, half_width), BF16),
            pltpu.VMEM((NZ, 16, half_width), BF16),
            pltpu.VMEM((2, NZ, 16, width), BF16),
            pltpu.VMEM((2, TOK, width), BF16),
            pltpu.VMEM((ROWS, 16, LANES), BF16),
            pltpu.VMEM((ROWS - 1, 16, LANES), BF16),
            pltpu.SemaphoreType.DMA((NUM_SEMS,)),
            pltpu.SemaphoreType.DMA((NUM_SEMS,)),
            pltpu.SemaphoreType.DMA((4,)),
        ],
        compiler_params=pltpu.CompilerParams(
            collective_id=0, has_side_effects=True, vmem_limit_bytes=48 * 1024 * 1024
        ),
        name="swiglu_step",
    )(target_rows, buckets, tokens, w_gate, w_up, w_down, target_table)


def solution(mesh):
    in_specs = (
        P("row", "col"),
        P("col", "row"),
        P("col", "row"),
        P("row", "col"),
        P(None, "col"),
        P("row"),
        P("row"),
    )
    out_specs = (
        P("row", "col"),
        P("row", "col"),
        P("col", "row"),
        P("col", "row"),
        P("row", "col"),
    )
    return jax.shard_map(
        on_device, mesh=mesh, in_specs=in_specs, out_specs=out_specs, check_vma=False
    )
```

time: 729 us -> 84.9 us (0.12)
  waiting for transfers between devices: 564 us -> 0 us
  blocking collectives: 129 us -> 0 us
  Pallas kernels: 0 us -> 73.8 us
  between operations: 13.9 us -> 0.66 us
  matrix products: 8.15 us -> 0 us
    reduce_scatter x4 -> x0, waiting for transfers between devices: 564 us -> none  [the longest x1 211 us: on_device(): lax.psum_scatter(jnp.dot(hidden, w_down, preferred_element_type=jnp.float...]
    all_gather x5 -> x0, blocking collectives: 129 us -> none  [the longest x1 38.8 us: on_device(): x_full = lax.all_gather(tokens, 'row', axis=0, tiled=True)]
    pallas_call x0 -> x1, Pallas kernels: none -> 73.8 us  [on_device(): pl.pallas_call(kernel, out_shape=tuple((jax.ShapeDtypeStruct(a.shape, BF1...]
    dot_general x10 -> x0, matrix products: 8.15 us -> none  [the longest x3 2.88 us: rhs_product(): lax.dot_general(left, right, (((1,), (1,)), ((), ())), preferred_element_...]
  transfers between devices with their start and end apart: 4 -> 0, of which waited for: 4 -> 0; matrix products, arithmetic and copies ran while one was open for 1% -> 0% of each run, Pallas kernels for 0% -> 0%
where the time goes in v1:
time: 84.9 us; the launch traced here: 84.6 us
  Pallas kernels  73.8 us (87%)
  local copies, waits for them, and re-layouts  10.1 us (12%)
    pallas_call x1, Pallas kernels, on_device(): pl.pallas_call(kernel, out_shape=tuple((jax.ShapeDtypeStruct(a.shape, BF1...  73.8 us
    unnamed x19, local copies, waits for them, and re-layouts  10.1 us

profile of v1, /device:TPU:1, one launch (start us, length us, event | category | flops | bytes accessed | tf_op | source)
XLA Modules:
  0.0 84.6 jit_solution(13370798712133830446)
XLA Ops:
  0.6 0.0 copy-start
  0.6 1.1 %copy-done = bf16[512,768]{1,0:T(8,128)(2,1)S(1)} copy-done((bf16[512,768]{1,0:T(8,128)(2,1)S(1)}, bf16[512,768]{1,0:T(8,128)(2,1)}, u32[]{:S(2)}) %copy-start) | copy-done | bytes 786456
  1.8 0.0 copy-start.1
  1.8 1.1 %copy-done.1 = bf16[512,768]{1,0:T(8,128)(2,1)S(1)} copy-done((bf16[512,768]{1,0:T(8,128)(2,1)S(1)}, bf16[512,768]{1,0:T(8,128)(2,1)}, u32[]{:S(2)}) %copy-start.1) | copy-done | bytes 786456
  2.9 0.0 copy-start.2
  2.9 1.1 %copy-done.2 = bf16[768,512]{1,0:T(8,128)(2,1)S(1)} copy-done((bf16[768,512]{1,0:T(8,128)(2,1)S(1)}, bf16[768,512]{1,0:T(8,128)(2,1)}, u32[]{:S(2)}) %copy-start.2) | copy-done | bytes 786456
  4.0 0.0 copy-start.3
  4.0 0.9 %copy-done.3 = bf16[128,512]{1,0:T(8,128)(2,1)S(1)} copy-done((bf16[128,512]{1,0:T(8,128)(2,1)S(1)}, bf16[128,512]{1,0:T(8,128)(2,1)}, u32[]{:S(2)}) %copy-start.3) | copy-done | bytes 131096
  4.9 0.0 copy-start.4
  4.9 0.7 copy-done.4
  5.6 0.0 copy-start.5
  5.6 0.7 copy-done.5
  6.3 0.0 copy-start.6
  6.3 0.7 copy-done.6
  6.9 73.8 %swiglu_step.1 = (bf16[8,512]{1,0:T(8,128)(2,1)S(1)}, bf16[8,512]{1,0:T(8,128)(2,1)S(1)}, bf16[512,768]{1,0:T(8,128)(2,1)S(1)}, bf16[512,768]{1,0:T(8,128)(2,1)S(1)}, bf16[768,512]{1,0:T(8,128)(2,1)S(1)}) custom-call(s32[4]{0:T(128)S(1)} %copy-done.5, s32[4]{0:T(128)S(1)} %copy-done.6, bf16[8,512]{1,0:T(8,128)(2,1)S(1)} %copy-done.4, ...), custom_call_target="tpu_custom_call" | custom-call | tf_op jit(solution)/shard_map/swiglu_step/pallas_call | solution.py:318
  80.8 0.6 copy.17
  81.4 0.6 copy.18
  82.0 0.9 %copy.19 = bf16[512,768]{1,0:T(8,128)(2,1)} copy(bf16[512,768]{1,0:T(8,128)(2,1)S(1)} %get-tuple-element.12) | data formatting | bytes 1572864
  82.8 0.9 %copy.20 = bf16[512,768]{1,0:T(8,128)(2,1)} copy(bf16[512,768]{1,0:T(8,128)(2,1)S(1)} %get-tuple-element.13) | data formatting | bytes 1572864
  83.7 0.9 %copy.21 = bf16[768,512]{1,0:T(8,128)(2,1)} copy(bf16[768,512]{1,0:T(8,128)(2,1)S(1)} %get-tuple-element.14) | data formatting | bytes 1572864
Async XLA Ops:
  0.6 1.1 %copy-start = (bf16[512,768]{1,0:T(8,128)(2,1)S(1)}, bf16[512,768]{1,0:T(8,128)(2,1)}, u32[]{:S(2)}) copy-start(bf16[512,768]{1,0:T(8,128)(2,1)} %wg_hbm.1) | copy-start | bytes 2359300
  1.8 1.1 %copy-start.1 = (bf16[512,768]{1,0:T(8,128)(2,1)S(1)}, bf16[512,768]{1,0:T(8,128)(2,1)}, u32[]{:S(2)}) copy-start(bf16[512,768]{1,0:T(8,128)(2,1)} %wu_hbm.1) | copy-start | bytes 2359300
  2.9 1.1 %copy-start.2 = (bf16[768,512]{1,0:T(8,128)(2,1)S(1)}, bf16[768,512]{1,0:T(8,128)(2,1)}, u32[]{:S(2)}) copy-start(bf16[768,512]{1,0:T(8,128)(2,1)} %wd_hbm.1) | copy-start | bytes 2359300
  4.0 0.9 %copy-start.3 = (bf16[128,512]{1,0:T(8,128)(2,1)S(1)}, bf16[128,512]{1,0:T(8,128)(2,1)}, u32[]{:S(2)}) copy-start(bf16[128,512]{1,0:T(8,128)(2,1)} %table_hbm.1) | copy-start | bytes 393220
  4.9 0.7 copy-start.4
  5.6 0.7 copy-start.5
  6.3 0.7 copy-start.6

commit v2 on v1

v2 whole, which is shorter than its diff:
```python
import jax
import jax.numpy as jnp
from jax import lax
from jax.experimental import pallas as pl
from jax.experimental.pallas import tpu as pltpu
from jax.sharding import PartitionSpec as P

VMEM_BYTES = 60 * 1024 * 1024
PIECES = 4
MESH = pl.DeviceIdType.MESH
BF16, F32 = jnp.bfloat16, jnp.float32

NY, NX, NZ = 8, 4, 8
ROWS = NY * NX
HALF = 4
LANES = 128
TOK = ROWS * HALF

(
    S_A0, S_A1, S_BP0, S_BP1, S_B0, S_B1, S_C0, S_C1, S_CP, S_D0, S_D1,
    S_E, S_EP, S_F, S_G, S_GP, S_H, S_WD, S_TG, S_Y, NUM_SEMS,
) = range(21)
PAIR = HALF // 2


def zigzag(m, n):
    half = (m + 1) // 2
    return n // 2 + jnp.where(m % 2 == 0, half, -half)


def dot(left, right, dims):
    return lax.dot_general(left, right, ((dims[0], dims[1]), ((), ())), preferred_element_type=F32)


def kernel(
    rows_hbm, buckets_hbm, tokens_hbm, wg_hbm, wu_hbm, wd_hbm, table_hbm,
    y_hbm, gt_hbm, gg_hbm, gu_hbm, gd_hbm,
    rows_s, buckets_s, tokens_ref, table, wg, wu, wd,
    xs, xr, f_in, x_mat,
    gu_part, gu_psend, gu_precv, gu_zsend, gu_zrecv, gu_keep,
    hc, h_mat,
    f_out, y_send, y_recv, y_keep, y_give, y_take, tgt, tgt_give,
    gy_send, gy_recv, gy_mat, gy_give,
    gh_zsend, gh_zrecv,
    ac, act_mat, gt_send, gt_recv,
    y_out, gt_out, gg_out, gu_out, gd_out,
    send_sem, recv_sem, load_sem, store_sem, pair_sem, act_sem,
):
    row, col = lax.axis_index("row"), lax.axis_index("col")
    y, x, z, k = row // NX, row % NX, col // 2, col % 2
    width = wg.shape[1]
    wide = wg.shape[0]
    chunks = wide // LANES
    half_width = width // 2

    loads = [
        pltpu.make_async_copy(src, dst, load_sem.at[i])
        for i, (src, dst) in enumerate(
            [
                (rows_hbm, rows_s), (buckets_hbm, buckets_s), (tokens_hbm, tokens_ref), (table_hbm, table),
                (wg_hbm, wg), (wu_hbm, wu), (wd_hbm, wd.at[k]),
            ]
        )
    ]
    for load in loads:
        load.start()

    stores = [
        pltpu.make_async_copy(src, dst, store_sem.at[i])
        for i, (src, dst) in enumerate(
            [(y_out, y_hbm), (gt_out, gt_hbm), (gg_out, gg_hbm), (gu_out, gu_hbm), (gd_out, gd_hbm)]
        )
    ]

    def row_peer(m, sign):
        dy, dx = zigzag(m // NX, NY), zigzag(m % NX, NX)
        return (((y + NY + sign * dy) % NY) * NX + (x + NX + sign * dx) % NX, col)

    def z_peer(m):
        return (z + zigzag(m, NZ)) % NZ

    partner = (row, z * 2 + 1 - k)

    barrier = pltpu.get_barrier_semaphore()

    def greet_row(m, carry):
        pl.semaphore_signal(barrier, inc=1, device_id=row_peer(m, 1), device_id_type=MESH)
        return carry

    def greet_col(m, carry):
        pl.semaphore_signal(barrier, inc=1, device_id=(row, z_peer(m) * 2 + k), device_id_type=MESH)
        return carry

    lax.fori_loop(0, ROWS - 1, greet_row, 0)
    lax.fori_loop(0, NZ - 1, greet_col, 0)
    pl.semaphore_signal(barrier, inc=1, device_id=partner, device_id_type=MESH)

    loads[0].wait()
    loads[2].wait()
    tgt_pos = [rows_s[i] - 2 * HALF * row for i in range(HALF)]
    rest_pos = [jnp.int32(0)] * HALF
    seen = jnp.int32(0)
    for t in range(2 * HALF):
        is_target = jnp.int32(0)
        for p in tgt_pos:
            is_target = is_target + jnp.where(p == t, 1, 0)
        for i in range(HALF):
            rest_pos[i] = rest_pos[i] + jnp.where(seen == i, 1 - is_target, 0) * t
        seen = seen + 1 - is_target
    pos = [tgt_pos, rest_pos]

    tok = tokens_ref[...].astype(F32)
    iota8 = lax.broadcasted_iota(jnp.int32, tok.shape, 0)
    iota16 = lax.broadcasted_iota(jnp.int32, (16, LANES), 0)
    for h in range(2):
        packed = jnp.zeros((16, LANES), F32)
        for i in range(HALF):
            line = jnp.sum(jnp.where(iota8 == pos[h][i], tok, 0.0), axis=0, keepdims=True)
            for j in range(chunks):
                piece = line[:, j * LANES : (j + 1) * LANES]
                packed = jnp.where(iota16 == j * HALF + i, piece, packed)
        xs[h] = packed.astype(BF16)
        xr[h, ROWS - 1] = packed.astype(BF16)

    loads[1].wait()
    loads[3].wait()
    targets = jnp.zeros((16, LANES), F32)
    lane16 = lax.broadcasted_iota(jnp.int32, (16, table.shape[0]), 1)
    sub16 = lax.broadcasted_iota(jnp.int32, (16, table.shape[0]), 0)
    for j in range(chunks):
        onehot = jnp.zeros((16, table.shape[0]), F32)
        for i in range(HALF):
            at = i // PAIR * 8 + j * PAIR + i % PAIR
            hit = jnp.logical_and(sub16 == at, lane16 == buckets_s[i])
            onehot = jnp.where(hit, 1.0, onehot)
        targets = targets + dot(onehot.astype(BF16), table[:, j * LANES : (j + 1) * LANES], ((1,), (0,)))
    first = (jnp.zeros((8, LANES), jnp.int32) + k) == 0
    tgt[k] = jnp.where(first, targets[0:8], targets[8:16])
    tgt_give[...] = jnp.where(first, targets[8:16], targets[0:8])

    pl.semaphore_wait(barrier, ROWS - 1 + NZ - 1 + 1)

    def wait_recv(ref, s):
        pltpu.make_async_copy(ref, ref, recv_sem.at[s]).wait()

    def wait_send(ref, s):
        pltpu.make_async_copy(ref, ref, send_sem.at[s]).wait()

    def remote(src, dst, s, device, arrived=None):
        pltpu.make_async_remote_copy(
            src_ref=src, dst_ref=dst, send_sem=send_sem.at[s],
            recv_sem=recv_sem.at[s] if arrived is None else arrived,
            device_id=device, device_id_type=MESH,
        ).start()

    def spread_rows(src, dst, s):
        def one(m, carry):
            remote(src, dst.at[m], s, row_peer(m, 1))
            return carry

        lax.fori_loop(0, ROWS - 1, one, 0)

    def scatter_rows(src, dst, s):
        def one(m, carry):
            remote(src.at[m], dst.at[m], s, row_peer(m, -1))
            return carry

        lax.fori_loop(0, ROWS - 1, one, 0)

    def scatter_z(src, dst, s):
        def one(m, carry):
            peer = z_peer(m)
            remote(src.at[peer], dst.at[z], s, (row, peer * 2 + k))
            return carry

        lax.fori_loop(0, NZ - 1, one, 0)

    def spread_z(buf, s, arrived=None):
        def one(m, carry):
            here = buf.at[k, z]
            remote(here, here, s, (row, z_peer(m) * 2 + k), None if arrived is None else arrived.at[m])
            return carry

        lax.fori_loop(0, NZ - 1, one, 0)

    def others(buf, n):
        return buf.at[pl.ds(0, n - 1)]

    def load_rows(buf):
        f_in[...] = buf[...].astype(F32).reshape(ROWS * 16, LANES)

    def columns(at, tokens):
        parts = [f_in[pl.ds(at + i, ROWS, stride=16), :] for i in range(tokens)]
        return jnp.concatenate(parts, axis=0).astype(BF16)

    def put_columns(mat, at, tokens):
        for i in range(tokens):
            f_out[pl.ds(at + i, ROWS, stride=16), :] = mat[i * ROWS : (i + 1) * ROWS]

    def store_rows(out):
        out[...] = f_out[...].reshape(ROWS, 16, LANES).astype(BF16)

    def part(j):
        return slice(j * LANES, (j + 1) * LANES)

    def own_total():
        return f_out[(ROWS - 1) * 16 : ROWS * 16, :]

    def place(values, iota, blocks):
        block = blocks
        for token, line in values:
            block = jnp.where(iota == token, line, block)
        return block

    def gate_up_part(h):
        load_rows(xr.at[h])
        for j in range(chunks):
            x_mat[h, :, part(j)] = columns(j * HALF, HALF)
        xm = x_mat[h]
        gate = dot(xm, wg[...], ((1,), (0,)))
        gu_part[:, :, 0:8, :] = gate.reshape(2, NZ, 8, width)
        up = dot(xm, wu[...], ((1,), (0,)))
        gu_part[:, :, 8:16, :] = up.reshape(2, NZ, 8, width)

        def give(m, carry):
            at = z_peer(m)
            gu_psend[h, at] = gu_part[1 - k, at].astype(BF16)
            remote(gu_psend.at[h, at], gu_precv.at[h, at], S_BP0 + h, partner, pair_sem.at[h, m])
            return carry

        lax.fori_loop(0, NZ, give, 0)

    def gate_up_scatter(h):
        def add(m):
            at = z_peer(m)
            pltpu.make_async_copy(gu_precv.at[h, 0], gu_precv.at[h, 0], pair_sem.at[h, m]).wait()
            return at, (gu_part[k, at] + gu_precv[h, at].astype(F32)).astype(BF16)

        def one(m, carry):
            at, total = add(m)
            gu_zsend[h, at] = total
            remote(gu_zsend.at[h, at], gu_zrecv.at[h, z], S_B0 + h, (row, at * 2 + k))
            return carry

        lax.fori_loop(0, NZ - 1, one, 0)
        gu_zrecv[h, z] = add(NZ - 1)[1]

    def hidden_spread(h):
        wait_recv(others(gu_zrecv.at[h], NZ), S_B0 + h)
        both = jnp.sum(gu_zrecv[h].astype(F32), axis=0)
        if h == 0:
            gu_keep[...] = both
        gate, up = both[0:8], both[8:16]
        hid = gate * jax.nn.sigmoid(gate) * up
        hc[h, k, z] = jnp.concatenate([hid[:, :half_width], hid[:, half_width:]], axis=0).astype(BF16)
        spread_z(hc.at[h], S_C0 + h)

    def hidden_matrix(h, core):
        v = hc[h, core].astype(F32)
        left = v[:, 0:8].reshape(TOK // 2, half_width).astype(BF16)
        right = v[:, 8:16].reshape(TOK // 2, half_width).astype(BF16)
        return jnp.concatenate([left, right], axis=1)

    def output_scatter(h):
        wait_recv(others(hc.at[h, 0], NZ), S_C0 + h)
        hm = hidden_matrix(h, k)
        if h == 0:
            h_mat[k] = hm
        for c in range(2):
            out = dot(hm, wd[c], ((1,), (0,)))
            for j in range(chunks):
                put_columns(out[:, part(j)], c * 8 + j * PAIR, PAIR)
        store_rows(y_send.at[h])
        y_keep[h] = own_total().reshape(2, 8, LANES)
        scatter_rows(y_send.at[h], y_recv.at[h], S_D0 + h)

    def output_total(h):
        wait_recv(y_recv.at[h], S_D0 + h)
        total = y_keep[h] + jnp.sum(y_recv[h].astype(F32), axis=0).reshape(2, 8, LANES)
        y_keep[h] = total.astype(BF16).astype(F32)

    spread_rows(xs.at[0], xr.at[0], S_A0)
    remote(tgt_give, tgt.at[k], S_TG, partner)
    for load in loads[4:]:
        load.wait()
    remote(wd.at[k], wd.at[k], S_WD, partner)
    wait_recv(others(xr.at[0], ROWS), S_A0)
    gate_up_part(0)
    gate_up_scatter(0)
    spread_rows(xs.at[1], xr.at[1], S_A1)
    hidden_spread(0)
    wait_recv(others(xr.at[1], ROWS), S_A1)
    gate_up_part(1)
    wait_recv(wd.at[0], S_WD)
    output_scatter(0)
    remote(hc.at[0, k], hc.at[0, k], S_CP, partner)
    gate_up_scatter(1)
    wait_recv(tgt_give, S_TG)
    output_total(0)

    gy = (0.25 * (y_keep[0] - tgt[...])).reshape(16, LANES).astype(BF16)
    gy_send[...] = gy
    gy_recv[ROWS - 1] = gy
    spread_rows(gy_send, gy_recv, S_E)
    hidden_spread(1)
    wait_recv(others(gy_recv, ROWS), S_E)

    load_rows(gy_recv)
    for j in range(chunks):
        gy_mat[k, :, part(j)] = columns(k * 8 + j * PAIR, PAIR)
        gy_give[:, part(j)] = columns((1 - k) * 8 + j * PAIR, PAIR)
    gh = dot(gy_mat[k], wd[k], ((1,), (1,))) + dot(gy_give[...], wd[1 - k], ((1,), (1,)))
    gh = gh.reshape(NZ, 8, width)
    gh = jnp.concatenate([gh[:, :, :half_width], gh[:, :, half_width:]], axis=1)
    gh_zsend[...] = gh.astype(BF16)
    gh_zrecv[z] = gh_zsend[z]
    scatter_z(gh_zsend, gh_zrecv, S_F)
    remote(gy_give, gy_mat.at[k], S_EP, partner)
    output_scatter(1)
    wait_recv(others(gh_zrecv, NZ), S_F)
    total = jnp.sum(gh_zrecv[...].astype(F32), axis=0)
    grad_hidden = jnp.concatenate([total[0:8], total[8:16]], axis=1)
    gate, up = gu_keep[0:8], gu_keep[8:16]
    sig = jax.nn.sigmoid(gate)
    gate_act = grad_hidden * up * sig * (1.0 + gate * (1.0 - sig))
    up_act = grad_hidden * gate * sig
    ac[k, z] = jnp.concatenate([gate_act, up_act], axis=0).astype(BF16)
    spread_z(ac, S_G, act_sem)
    remote(ac.at[k, z], ac.at[k, z], S_GP, partner)

    wait_recv(hc.at[0, 0], S_CP)
    wait_recv(gy_give, S_EP)
    h_mat[1 - k] = hidden_matrix(0, 1 - k)
    gd_out[...] = dot(
        h_mat[...].reshape(TOK, width), gy_mat[...].reshape(TOK, wide), ((0,), (0,))
    ).astype(BF16)
    stores[4].start()

    def pass_on(n, carry):
        m = NZ - 2 - n
        at = (z + NZ - zigzag(m, NZ)) % NZ
        pltpu.make_async_copy(ac.at[0, 0], ac.at[0, 0], act_sem.at[m]).wait()
        remote(ac.at[k, at], ac.at[k, at], S_GP, partner)
        return carry

    lax.fori_loop(0, NZ - 1, pass_on, 0)
    wait_recv(ac.at[0], S_GP)
    v = ac[...].astype(F32).reshape(2 * NZ, 16, width)
    act_mat[0] = v[:, 0:8].reshape(TOK, width).astype(BF16)
    act_mat[1] = v[:, 8:16].reshape(TOK, width).astype(BF16)
    grad = dot(act_mat[0], wg[...], ((1,), (1,))) + dot(act_mat[1], wu[...], ((1,), (1,)))
    for j in range(chunks):
        put_columns(grad[:, part(j)], j * HALF, HALF)
    store_rows(gt_send)
    scatter_rows(gt_send, gt_recv, S_H)

    output_total(1)
    for h in range(2):
        y_give[h] = y_keep[h, 1 - k]
    remote(y_give, y_take, S_Y, partner)
    gg_out[...] = dot(x_mat[0], act_mat[0], ((0,), (0,))).astype(BF16)
    stores[2].start()
    gu_out[...] = dot(x_mat[0], act_mat[1], ((0,), (0,))).astype(BF16)
    stores[3].start()
    wait_recv(y_give, S_Y)
    iota_t = lax.broadcasted_iota(jnp.int32, (2 * HALF, LANES), 0)
    zero = jnp.zeros((2 * HALF, LANES), F32)
    own, taken = [y_keep[h, k] for h in range(2)], [y_take[h] for h in range(2)]
    for j in range(chunks):
        values = []
        for h in range(2):
            for i in range(PAIR):
                at = j * PAIR + i
                low, high = pos[h][i], pos[h][PAIR + i]
                values.append((jnp.where(k == 0, low, high), own[h][at : at + 1]))
                values.append((jnp.where(k == 0, high, low), taken[h][at : at + 1]))
        y_out[:, part(j)] = place(values, iota_t, zero).astype(BF16)
    stores[0].start()
    wait_recv(gt_recv, S_H)
    total = own_total() + jnp.sum(gt_recv[...].astype(F32), axis=0)
    for j in range(chunks):
        values = [(pos[0][i], total[j * HALF + i : j * HALF + i + 1]) for i in range(HALF)]
        gt_out[:, part(j)] = place(values, iota_t, zero).astype(BF16)
    stores[1].start()

    for h in range(2):
        wait_send(others(xr.at[h], ROWS), S_A0 + h)
        wait_send(gu_precv.at[h], S_BP0 + h)
        wait_send(others(gu_zrecv.at[h], NZ), S_B0 + h)
        wait_send(others(hc.at[h, 0], NZ), S_C0 + h)
        wait_send(y_recv.at[h], S_D0 + h)
    wait_send(tgt_give, S_TG)
    wait_send(wd.at[0], S_WD)
    wait_send(hc.at[0, 0], S_CP)
    wait_send(others(gy_recv, ROWS), S_E)
    wait_send(gy_give, S_EP)
    wait_send(others(gh_zrecv, NZ), S_F)
    wait_send(others(ac.at[0], NZ), S_G)
    wait_send(ac.at[0], S_GP)
    wait_send(y_give, S_Y)
    wait_send(gt_recv, S_H)
    for store in stores:
        store.wait()


def write_out(*refs):
    sources, results, held, sem_in, sem_out = refs[0:5], refs[5:10], refs[10:15], refs[15], refs[16]
    reads, writes = [], []
    for src, dst, buf in zip(sources, results, held):
        rows = src.shape[0]
        step = rows // PIECES if rows >= 16 * PIECES else rows
        for at in range(0, rows, step):
            rng = pl.ds(at, step)
            n = len(reads)
            reads.append(pltpu.make_async_copy(src.at[rng], buf.at[rng], sem_in.at[n]))
            writes.append(pltpu.make_async_copy(buf.at[rng], dst.at[rng], sem_out.at[n]))
    for read in reads:
        read.start()
    for read, write in zip(reads, writes):
        read.wait()
        write.start()
    for write in writes:
        write.wait()


def on_device(tokens, w_gate, w_up, w_down, target_table, target_rows, buckets):
    wide, width = w_gate.shape
    half_width = width // 2
    hbm = pl.BlockSpec(memory_space=pltpu.HBM)
    outs = (tokens, tokens, w_gate, w_up, w_down)
    results = pl.pallas_call(
        kernel,
        out_shape=tuple(jax.ShapeDtypeStruct(a.shape, BF16) for a in outs),
        in_specs=[hbm] * 7,
        out_specs=(hbm,) * 5,
        scratch_shapes=[
            pltpu.SMEM(target_rows.shape, jnp.int32),
            pltpu.SMEM(buckets.shape, jnp.int32),
            pltpu.VMEM(tokens.shape, BF16),
            pltpu.VMEM(target_table.shape, BF16),
            pltpu.VMEM(w_gate.shape, BF16),
            pltpu.VMEM(w_up.shape, BF16),
            pltpu.VMEM((2, *w_down.shape), BF16),
            pltpu.VMEM((2, 16, LANES), BF16),
            pltpu.VMEM((2, ROWS, 16, LANES), BF16),
            pltpu.VMEM((ROWS * 16, LANES), F32),
            pltpu.VMEM((2, TOK, wide), BF16),
            pltpu.VMEM((2, NZ, 16, width), F32),
            pltpu.VMEM((2, NZ, 16, width), BF16),
            pltpu.VMEM((2, NZ, 16, width), BF16),
            pltpu.VMEM((2, NZ, 16, width), BF16),
            pltpu.VMEM((2, NZ, 16, width), BF16),
            pltpu.VMEM((16, width), F32),
            pltpu.VMEM((2, 2, NZ, 16, half_width), BF16),
            pltpu.VMEM((2, TOK // 2, width), BF16),
            pltpu.VMEM((ROWS * 16, LANES), F32),
            pltpu.VMEM((2, ROWS, 16, LANES), BF16),
            pltpu.VMEM((2, ROWS - 1, 16, LANES), BF16),
            pltpu.VMEM((2, 2, 8, LANES), F32),
            pltpu.VMEM((2, 8, LANES), F32),
            pltpu.VMEM((2, 8, LANES), F32),
            pltpu.VMEM((2, 8, LANES), F32),
            pltpu.VMEM((8, LANES), F32),
            pltpu.VMEM((16, LANES), BF16),
            pltpu.VMEM((ROWS, 16, LANES), BF16),
            pltpu.VMEM((2, TOK // 2, wide), BF16),
            pltpu.VMEM((TOK // 2, wide), BF16),
            pltpu.VMEM((NZ, 16, half_width), BF16),
            pltpu.VMEM((NZ, 16, half_width), BF16),
            pltpu.VMEM((2, NZ, 16, width), BF16),
            pltpu.VMEM((2, TOK, width), BF16),
            pltpu.VMEM((ROWS, 16, LANES), BF16),
            pltpu.VMEM((ROWS - 1, 16, LANES), BF16),
            *(pltpu.VMEM(a.shape, BF16) for a in outs),
            pltpu.SemaphoreType.DMA((NUM_SEMS,)),
            pltpu.SemaphoreType.DMA((NUM_SEMS,)),
            pltpu.SemaphoreType.DMA((7,)),
            pltpu.SemaphoreType.DMA((5,)),
            pltpu.SemaphoreType.DMA((2, NZ)),
            pltpu.SemaphoreType.DMA((NZ - 1,)),
        ],
        compiler_params=pltpu.CompilerParams(
            collective_id=0, has_side_effects=True, vmem_limit_bytes=VMEM_BYTES
        ),
        name="swiglu_step",
    )(target_rows, buckets, tokens, w_gate, w_up, w_down, target_table)
    return pl.pallas_call(
        write_out,
        out_shape=tuple(jax.ShapeDtypeStruct(a.shape, BF16) for a in outs),
        in_specs=[hbm] * 5,
        out_specs=(hbm,) * 5,
        scratch_shapes=[
            *(pltpu.VMEM(a.shape, BF16) for a in outs),
            pltpu.SemaphoreType.DMA((5 * PIECES,)),
            pltpu.SemaphoreType.DMA((5 * PIECES,)),
        ],
        compiler_params=pltpu.CompilerParams(vmem_limit_bytes=VMEM_BYTES),
        name="write_out",
    )(*results)


def solution(mesh):
    in_specs = (
        P("row", "col"),
        P("col", "row"),
        P("col", "row"),
        P("row", "col"),
        P(None, "col"),
        P("row"),
        P("row"),
    )
    out_specs = (
        P("row", "col"),
        P("row", "col"),
        P("col", "row"),
        P("col", "row"),
        P("row", "col"),
    )
    return jax.shard_map(
        on_device, mesh=mesh, in_specs=in_specs, out_specs=out_specs, check_vma=False
    )
```

time: 84.9 us -> 73 us (0.86)
  local copies, waits for them, and re-layouts: 10.1 us -> 0 us
  Pallas kernels: 73.8 us -> 72.2 us
    unnamed x19 -> x0, local copies, waits for them, and re-layouts: 10.1 us -> none
    pallas_call x1, Pallas kernels: 73.8 us -> 69.4 us  [on_device(): pl.pallas_call(kernel, out_shape=tuple((jax.ShapeDtypeStruct(a.shape, BF1...]
    pallas_call x0 -> x1, Pallas kernels: none -> 2.79 us  [on_device(): pl.pallas_call(write_out, out_shape=tuple((jax.ShapeDtypeStruct(a.shape,...]
where the time goes in v2:
time: 73 us; the launch traced here: 72.8 us
  Pallas kernels  72.2 us (99%)
    pallas_call x1, Pallas kernels, on_device(): pl.pallas_call(kernel, out_shape=tuple((jax.ShapeDtypeStruct(a.shape, BF1...  69.4 us
    pallas_call x1, Pallas kernels, on_device(): pl.pallas_call(write_out, out_shape=tuple((jax.ShapeDtypeStruct(a.shape,...  2.79 us

profile of v2, /device:TPU:1, one launch (start us, length us, event | category | flops | bytes accessed | tf_op | source)
XLA Modules:
  0.0 72.8 jit_solution(16583129384083304206)
XLA Ops:
  0.6 69.4 %swiglu_step.1 = (bf16[8,512]{1,0:T(8,128)(2,1)}, bf16[8,512]{1,0:T(8,128)(2,1)}, bf16[512,768]{1,0:T(8,128)(2,1)}, bf16[512,768]{1,0:T(8,128)(2,1)}, bf16[768,512]{1,0:T(8,128)(2,1)}) custom-call(s32[4]{0:T(128)} %rows_hbm.1, s32[4]{0:T(128)} %buckets_hbm.1, bf16[8,512]{1,0:T(8,128)(2,1)} %tokens_hbm.1, bf16[512,768]{1,0:T(8,128)(2,1)} %wg_hbm.1, ...), custom_call_target="tpu_custom_call" | custom-call | tf_op jit(solution)/shard_map/swiglu_step/pallas_call | solution.py:431
  70.1 2.8 %write_out.1 = (bf16[8,512]{1,0:T(8,128)(2,1)}, bf16[8,512]{1,0:T(8,128)(2,1)}, bf16[512,768]{1,0:T(8,128)(2,1)}, bf16[512,768]{1,0:T(8,128)(2,1)}, bf16[768,512]{1,0:T(8,128)(2,1)}) custom-call(bf16[8,512]{1,0:T(8,128)(2,1)} %get-tuple-element.10.refs_0_, bf16[8,512]{1,0:T(8,128)(2,1)} %get-tuple-element.11.refs_1_, ...), custom_call_target="tpu_custom_call" | custom-call | tf_op jit(solution)/shard_map/write_out/pallas_call | solution.py:487

commit v3 on v2

--- a/solution.py
+++ b/solution.py
@@ -17,9 +17,9 @@
 TOK = ROWS * HALF
 
 (
-    S_A0, S_A1, S_BP0, S_BP1, S_B0, S_B1, S_C0, S_C1, S_CP, S_D0, S_D1,
-    S_E, S_EP, S_F, S_G, S_GP, S_H, S_WD, S_TG, S_Y, NUM_SEMS,
-) = range(21)
+    S_A0, S_A1, S_AO0, S_AO1, S_B0, S_B1, S_C0, S_C1, S_CP, S_D0, S_D1,
+    S_E, S_EP, S_F, S_G, S_H, S_HO, S_WG, S_WU, S_WD, S_TG, S_Y, S_FC, S_X, S_AG, S_AU, NUM_SEMS,
+) = range(27)
 PAIR = HALF // 2
 
 
@@ -37,19 +37,18 @@
     y_hbm, gt_hbm, gg_hbm, gu_hbm, gd_hbm,
     rows_s, buckets_s, tokens_ref, table, wg, wu, wd,
     xs, xr, f_in, x_mat,
-    gu_part, gu_psend, gu_precv, gu_zsend, gu_zrecv, gu_keep,
+    x_full, gu_zsend, gu_zrecv,
     hc, h_mat,
     f_out, y_send, y_recv, y_keep, y_give, y_take, tgt, tgt_give,
-    gy_send, gy_recv, gy_mat, gy_give,
+    gy_send, gy_recv, gy_half, gy_mat,
     gh_zsend, gh_zrecv,
-    ac, act_mat, gt_send, gt_recv,
+    fc, factor, ghc, act_mat, gt_send, gt_recv,
     y_out, gt_out, gg_out, gu_out, gd_out,
-    send_sem, recv_sem, load_sem, store_sem, pair_sem, act_sem,
+    send_sem, recv_sem, load_sem, store_sem,
 ):
     row, col = lax.axis_index("row"), lax.axis_index("col")
     y, x, z, k = row // NX, row % NX, col // 2, col % 2
-    width = wg.shape[1]
-    wide = wg.shape[0]
+    wide, width = wg.shape[1:]
     chunks = wide // LANES
     half_width = width // 2
 
@@ -58,12 +57,12 @@
         for i, (src, dst) in enumerate(
             [
                 (rows_hbm, rows_s), (buckets_hbm, buckets_s), (tokens_hbm, tokens_ref), (table_hbm, table),
-                (wg_hbm, wg), (wu_hbm, wu), (wd_hbm, wd.at[k]),
+                (wg_hbm, wg.at[k]), (wu_hbm, wu.at[k]), (wd_hbm, wd.at[k]),
             ]
         )
     ]
-    for load in loads:
-        load.start()
+    loads[0].start()
+    loads[2].start()
 
     stores = [
         pltpu.make_async_copy(src, dst, store_sem.at[i])
@@ -72,9 +71,10 @@
         )
     ]
 
-    def row_peer(m, sign):
+    def row_peer(m, sign, core=None):
         dy, dx = zigzag(m // NX, NY), zigzag(m % NX, NX)
-        return (((y + NY + sign * dy) % NY) * NX + (x + NX + sign * dx) % NX, col)
+        column = col if core is None else z * 2 + core
+        return (((y + NY + sign * dy) % NY) * NX + (x + NX + sign * dx) % NX, column)
 
     def z_peer(m):
         return (z + zigzag(m, NZ)) % NZ
@@ -84,6 +84,7 @@
     barrier = pltpu.get_barrier_semaphore()
 
     def greet_row(m, carry):
+        pl.semaphore_signal(barrier, inc=1, device_id=row_peer(m, 1, 1 - k), device_id_type=MESH)
         pl.semaphore_signal(barrier, inc=1, device_id=row_peer(m, 1), device_id_type=MESH)
         return carry
 
@@ -95,6 +96,8 @@
     lax.fori_loop(0, NZ - 1, greet_col, 0)
     pl.semaphore_signal(barrier, inc=1, device_id=partner, device_id_type=MESH)
 
+    for i in (1, 3, 4, 5, 6):
+        loads[i].start()
     loads[0].wait()
     loads[2].wait()
     tgt_pos = [rows_s[i] - 2 * HALF * row for i in range(HALF)]
@@ -118,9 +121,10 @@
             line = jnp.sum(jnp.where(iota8 == pos[h][i], tok, 0.0), axis=0, keepdims=True)
             for j in range(chunks):
                 piece = line[:, j * LANES : (j + 1) * LANES]
-                packed = jnp.where(iota16 == j * HALF + i, piece, packed)
-        xs[h] = packed.astype(BF16)
-        xr[h, ROWS - 1] = packed.astype(BF16)
+                packed = jnp.where(iota16 == i // PAIR * 8 + j * PAIR + i % PAIR, piece, packed)
+        for c in range(2):
+            xs[h, c] = packed[c * 8 : c * 8 + 8].astype(BF16)
+        xr[h, k, ROWS - 1] = xs[h, k]
 
     loads[1].wait()
     loads[3].wait()
@@ -138,7 +142,7 @@
     tgt[k] = jnp.where(first, targets[0:8], targets[8:16])
     tgt_give[...] = jnp.where(first, targets[8:16], targets[0:8])
 
-    pl.semaphore_wait(barrier, ROWS - 1 + NZ - 1 + 1)
+    pl.semaphore_wait(barrier, 2 * (ROWS - 1) + NZ - 1 + 1)
 
     def wait_recv(ref, s):
         pltpu.make_async_copy(ref, ref, recv_sem.at[s]).wait()
@@ -146,10 +150,9 @@
     def wait_send(ref, s):
         pltpu.make_async_copy(ref, ref, send_sem.at[s]).wait()
 
-    def remote(src, dst, s, device, arrived=None):
+    def remote(src, dst, s, device):
         pltpu.make_async_remote_copy(
-            src_ref=src, dst_ref=dst, send_sem=send_sem.at[s],
-            recv_sem=recv_sem.at[s] if arrived is None else arrived,
+            src_ref=src, dst_ref=dst, send_sem=send_sem.at[s], recv_sem=recv_sem.at[s],
             device_id=device, device_id_type=MESH,
         ).start()
 
@@ -175,10 +178,10 @@
 
         lax.fori_loop(0, NZ - 1, one, 0)
 
-    def spread_z(buf, s, arrived=None):
+    def spread_z(buf, s):
         def one(m, carry):
             here = buf.at[k, z]
-            remote(here, here, s, (row, z_peer(m) * 2 + k), None if arrived is None else arrived.at[m])
+            remote(here, here, s, (row, z_peer(m) * 2 + k))
             return carry
 
         lax.fori_loop(0, NZ - 1, one, 0)
@@ -189,16 +192,13 @@
     def load_rows(buf):
         f_in[...] = buf[...].astype(F32).reshape(ROWS * 16, LANES)
 
-    def columns(at, tokens):
-        parts = [f_in[pl.ds(at + i, ROWS, stride=16), :] for i in range(tokens)]
+    def columns(at, step):
+        parts = [f_in[pl.ds(at + i, ROWS, stride=step), :] for i in range(PAIR)]
         return jnp.concatenate(parts, axis=0).astype(BF16)
 
-    def put_columns(mat, at, tokens):
-        for i in range(tokens):
-            f_out[pl.ds(at + i, ROWS, stride=16), :] = mat[i * ROWS : (i + 1) * ROWS]
-
-    def store_rows(out):
-        out[...] = f_out[...].reshape(ROWS, 16, LANES).astype(BF16)
+    def put_columns(mat, at, step):
+        for i in range(PAIR):
+            f_out[pl.ds(at + i, ROWS, stride=step), :] = mat[i * ROWS : (i + 1) * ROWS]
 
     def part(j):
         return slice(j * LANES, (j + 1) * LANES)
@@ -212,48 +212,43 @@
             block = jnp.where(iota == token, line, block)
         return block
 
-    def gate_up_part(h):
+    def tokens_spread(h):
+        def one(m, carry):
+            remote(xs.at[h, 1 - k], xr.at[h, k, m], S_AO0 + h, row_peer(m, 1, 1 - k))
+            remote(xs.at[h, k], xr.at[h, k, m], S_A0 + h, row_peer(m, 1))
+            return carry
+
+        lax.fori_loop(0, ROWS - 1, one, 0)
+        remote(xs.at[h, 1 - k], xr.at[h, k, ROWS - 1], S_AO0 + h, partner)
+
+    def tokens_wait(h):
+        wait_recv(others(xr.at[h, 0], ROWS), S_A0 + h)
+        wait_recv(xr.at[h, 0], S_AO0 + h)
+
+    def gate_up_scatter(h):
         load_rows(xr.at[h])
-        for j in range(chunks):
-            x_mat[h, :, part(j)] = columns(j * HALF, HALF)
-        xm = x_mat[h]
-        gate = dot(xm, wg[...], ((1,), (0,)))
-        gu_part[:, :, 0:8, :] = gate.reshape(2, NZ, 8, width)
-        up = dot(xm, wu[...], ((1,), (0,)))
-        gu_part[:, :, 8:16, :] = up.reshape(2, NZ, 8, width)
-
-        def give(m, carry):
-            at = z_peer(m)
-            gu_psend[h, at] = gu_part[1 - k, at].astype(BF16)
-            remote(gu_psend.at[h, at], gu_precv.at[h, at], S_BP0 + h, partner, pair_sem.at[h, m])
-            return carry
-
-        lax.fori_loop(0, NZ, give, 0)
-
-    def gate_up_scatter(h):
-        def add(m):
-            at = z_peer(m)
-            pltpu.make_async_copy(gu_precv.at[h, 0], gu_precv.at[h, 0], pair_sem.at[h, m]).wait()
-            return at, (gu_part[k, at] + gu_precv[h, at].astype(F32)).astype(BF16)
-
-        def one(m, carry):
-            at, total = add(m)
-            gu_zsend[h, at] = total
-            remote(gu_zsend.at[h, at], gu_zrecv.at[h, z], S_B0 + h, (row, at * 2 + k))
-            return carry
-
-        lax.fori_loop(0, NZ - 1, one, 0)
-        gu_zrecv[h, z] = add(NZ - 1)[1]
+        for c in range(2):
+            for j in range(chunks):
+                x_mat[h, c, :, part(j)] = columns(c * ROWS * 8 + j * PAIR, 8)
+        gate = dot(x_mat[h, 0], wg[0], ((1,), (0,))) + dot(x_mat[h, 1], wg[1], ((1,), (0,)))
+        up = dot(x_mat[h, 0], wu[0], ((1,), (0,))) + dot(x_mat[h, 1], wu[1], ((1,), (0,)))
+        gu_zsend[h, :, 0:16, :] = jnp.concatenate(
+            [gate.reshape(NZ, 8, width), up.reshape(NZ, 8, width)], axis=1
+        ).astype(BF16)
+        gu_zrecv[h, z] = gu_zsend[h, z]
+        scatter_z(gu_zsend.at[h], gu_zrecv.at[h], S_B0 + h)
 
     def hidden_spread(h):
         wait_recv(others(gu_zrecv.at[h], NZ), S_B0 + h)
         both = jnp.sum(gu_zrecv[h].astype(F32), axis=0)
-        if h == 0:
-            gu_keep[...] = both
         gate, up = both[0:8], both[8:16]
-        hid = gate * jax.nn.sigmoid(gate) * up
+        sig = jax.nn.sigmoid(gate)
+        hid = gate * sig * up
         hc[h, k, z] = jnp.concatenate([hid[:, :half_width], hid[:, half_width:]], axis=0).astype(BF16)
         spread_z(hc.at[h], S_C0 + h)
+        if h == 0:
+            gate_factor = up * sig * (1.0 + gate * (1.0 - sig))
+            fc[k, z] = jnp.concatenate([gate_factor, gate * sig], axis=0).astype(BF16)
 
     def hidden_matrix(h, core):
         v = hc[h, core].astype(F32)
@@ -269,8 +264,8 @@
         for c in range(2):
             out = dot(hm, wd[c], ((1,), (0,)))
             for j in range(chunks):
-                put_columns(out[:, part(j)], c * 8 + j * PAIR, PAIR)
-        store_rows(y_send.at[h])
+                put_columns(out[:, part(j)], c * 8 + j * PAIR, 16)
+        y_send[h] = f_out[...].reshape(ROWS, 16, LANES).astype(BF16)
         y_keep[h] = own_total().reshape(2, 8, LANES)
         scatter_rows(y_send.at[h], y_recv.at[h], S_D0 + h)
 
@@ -279,21 +274,26 @@
         total = y_keep[h] + jnp.sum(y_recv[h].astype(F32), axis=0).reshape(2, 8, LANES)
         y_keep[h] = total.astype(BF16).astype(F32)
 
-    spread_rows(xs.at[0], xr.at[0], S_A0)
+    tokens_spread(0)
     remote(tgt_give, tgt.at[k], S_TG, partner)
     for load in loads[4:]:
         load.wait()
+    remote(wg.at[k], wg.at[k], S_WG, partner)
+    remote(wu.at[k], wu.at[k], S_WU, partner)
     remote(wd.at[k], wd.at[k], S_WD, partner)
-    wait_recv(others(xr.at[0], ROWS), S_A0)
-    gate_up_part(0)
+    tokens_wait(0)
+    wait_recv(wg.at[0], S_WG)
+    wait_recv(wu.at[0], S_WU)
     gate_up_scatter(0)
-    spread_rows(xs.at[1], xr.at[1], S_A1)
+    tokens_spread(1)
+    x_full[k] = x_mat[0, k]
+    remote(x_mat.at[0, 1 - k], x_full.at[k], S_X, partner)
     hidden_spread(0)
-    wait_recv(others(xr.at[1], ROWS), S_A1)
-    gate_up_part(1)
+    tokens_wait(1)
     wait_recv(wd.at[0], S_WD)
     output_scatter(0)
     remote(hc.at[0, k], hc.at[0, k], S_CP, partner)
+    spread_z(fc, S_FC)
     gate_up_scatter(1)
     wait_recv(tgt_give, S_TG)
     output_total(0)
@@ -307,60 +307,69 @@
 
     load_rows(gy_recv)
     for j in range(chunks):
-        gy_mat[k, :, part(j)] = columns(k * 8 + j * PAIR, PAIR)
-        gy_give[:, part(j)] = columns((1 - k) * 8 + j * PAIR, PAIR)
-    gh = dot(gy_mat[k], wd[k], ((1,), (1,))) + dot(gy_give[...], wd[1 - k], ((1,), (1,)))
+        for c in range(2):
+            gy_half[c, :, part(j)] = columns(c * 8 + j * PAIR, 16)
+    gh = dot(gy_half[0], wd[0], ((1,), (1,))) + dot(gy_half[1], wd[1], ((1,), (1,)))
     gh = gh.reshape(NZ, 8, width)
     gh = jnp.concatenate([gh[:, :, :half_width], gh[:, :, half_width:]], axis=1)
     gh_zsend[...] = gh.astype(BF16)
     gh_zrecv[z] = gh_zsend[z]
     scatter_z(gh_zsend, gh_zrecv, S_F)
-    remote(gy_give, gy_mat.at[k], S_EP, partner)
+    remote(gy_half.at[1 - k], gy_mat.at[k], S_EP, partner)
+    gy_mat[k] = gy_half[k]
+    wait_recv(others(fc.at[0], NZ), S_FC)
+    v = fc[k].astype(F32)
+    factor[0] = v[:, 0:8].reshape(TOK // 2, width)
+    factor[1] = v[:, 8:16].reshape(TOK // 2, width)
+    wait_recv(others(gh_zrecv, NZ), S_F)
+    ghc[k, z] = jnp.sum(gh_zrecv[...].astype(F32), axis=0).astype(BF16)
+    spread_z(ghc, S_G)
+
     output_scatter(1)
-    wait_recv(others(gh_zrecv, NZ), S_F)
-    total = jnp.sum(gh_zrecv[...].astype(F32), axis=0)
-    grad_hidden = jnp.concatenate([total[0:8], total[8:16]], axis=1)
-    gate, up = gu_keep[0:8], gu_keep[8:16]
-    sig = jax.nn.sigmoid(gate)
-    gate_act = grad_hidden * up * sig * (1.0 + gate * (1.0 - sig))
-    up_act = grad_hidden * gate * sig
-    ac[k, z] = jnp.concatenate([gate_act, up_act], axis=0).astype(BF16)
-    spread_z(ac, S_G, act_sem)
-    remote(ac.at[k, z], ac.at[k, z], S_GP, partner)
+
+    wait_recv(others(ghc.at[0], NZ), S_G)
+    v = ghc[k].astype(F32)
+    for half in range(2):
+        grad_hidden = v[:, half * 8 : half * 8 + 8].reshape(TOK // 2, half_width)
+        cols = slice(half * half_width, (half + 1) * half_width)
+        for i in range(2):
+            act_mat[i, k, :, cols] = (grad_hidden * factor[i, :, cols]).astype(BF16)
+    gate_act, up_act = act_mat[0, k], act_mat[1, k]
+    for c in range(2):
+        grad = dot(gate_act, wg[c], ((1,), (1,))) + dot(up_act, wu[c], ((1,), (1,)))
+        for j in range(chunks):
+            put_columns(grad[:, part(j)], c * ROWS * 8 + j * PAIR, 8)
+    gt_send[...] = f_out[...].reshape(2, ROWS, 8, LANES).astype(BF16)
+    gt_recv[k, ROWS - 1] = gt_send[k, ROWS - 1]
+
+    def grad_out(m, carry):
+        remote(gt_send.at[1 - k, m], gt_recv.at[k, m], S_HO, row_peer(m, -1, 1 - k))
+        remote(gt_send.at[k, m], gt_recv.at[k, m], S_H, row_peer(m, -1))
+        return carry
+
+    lax.fori_loop(0, ROWS - 1, grad_out, 0)
+    remote(gt_send.at[1 - k, ROWS - 1], gt_recv.at[k, ROWS - 1], S_HO, partner)
+    remote(act_mat.at[0, k], act_mat.at[0, k], S_AG, partner)
+    remote(act_mat.at[1, k], act_mat.at[1, k], S_AU, partner)
 
     wait_recv(hc.at[0, 0], S_CP)
-    wait_recv(gy_give, S_EP)
+    wait_recv(gy_mat.at[0], S_EP)
     h_mat[1 - k] = hidden_matrix(0, 1 - k)
     gd_out[...] = dot(
         h_mat[...].reshape(TOK, width), gy_mat[...].reshape(TOK, wide), ((0,), (0,))
     ).astype(BF16)
     stores[4].start()
-
-    def pass_on(n, carry):
-        m = NZ - 2 - n
-        at = (z + NZ - zigzag(m, NZ)) % NZ
-        pltpu.make_async_copy(ac.at[0, 0], ac.at[0, 0], act_sem.at[m]).wait()
-        remote(ac.at[k, at], ac.at[k, at], S_GP, partner)
-        return carry
-
-    lax.fori_loop(0, NZ - 1, pass_on, 0)
-    wait_recv(ac.at[0], S_GP)
-    v = ac[...].astype(F32).reshape(2 * NZ, 16, width)
-    act_mat[0] = v[:, 0:8].reshape(TOK, width).astype(BF16)
-    act_mat[1] = v[:, 8:16].reshape(TOK, width).astype(BF16)
-    grad = dot(act_mat[0], wg[...], ((1,), (1,))) + dot(act_mat[1], wu[...], ((1,), (1,)))
-    for j in range(chunks):
-        put_columns(grad[:, part(j)], j * HALF, HALF)
-    store_rows(gt_send)
-    scatter_rows(gt_send, gt_recv, S_H)
-
     output_total(1)
     for h in range(2):
         y_give[h] = y_keep[h, 1 - k]
     remote(y_give, y_take, S_Y, partner)
-    gg_out[...] = dot(x_mat[0], act_mat[0], ((0,), (0,))).astype(BF16)
+    wait_recv(x_full.at[0], S_X)
+    wait_recv(act_mat.at[0, 0], S_AG)
+    wait_recv(act_mat.at[1, 0], S_AU)
+    xm = x_full[...].reshape(TOK, wide)
+    gg_out[...] = dot(xm, act_mat[0].reshape(TOK, width), ((0,), (0,))).astype(BF16)
     stores[2].start()
-    gu_out[...] = dot(x_mat[0], act_mat[1], ((0,), (0,))).astype(BF16)
+    gu_out[...] = dot(xm, act_mat[1].reshape(TOK, width), ((0,), (0,))).astype(BF16)
     stores[3].start()
     wait_recv(y_give, S_Y)
     iota_t = lax.broadcasted_iota(jnp.int32, (2 * HALF, LANES), 0)
@@ -376,16 +385,20 @@
                 values.append((jnp.where(k == 0, high, low), taken[h][at : at + 1]))
         y_out[:, part(j)] = place(values, iota_t, zero).astype(BF16)
     stores[0].start()
-    wait_recv(gt_recv, S_H)
-    total = own_total() + jnp.sum(gt_recv[...].astype(F32), axis=0)
+    wait_recv(others(gt_recv.at[0], ROWS), S_H)
+    wait_recv(gt_recv.at[0], S_HO)
+    totals = [jnp.sum(gt_recv[c].astype(F32), axis=0) for c in range(2)]
     for j in range(chunks):
-        values = [(pos[0][i], total[j * HALF + i : j * HALF + i + 1]) for i in range(HALF)]
+        values = []
+        for i in range(HALF):
+            at = j * PAIR + i % PAIR
+            values.append((pos[0][i], totals[i // PAIR][at : at + 1]))
         gt_out[:, part(j)] = place(values, iota_t, zero).astype(BF16)
     stores[1].start()
 
     for h in range(2):
-        wait_send(others(xr.at[h], ROWS), S_A0 + h)
-        wait_send(gu_precv.at[h], S_BP0 + h)
+        wait_send(others(xr.at[h, 0], ROWS), S_A0 + h)
+        wait_send(xr.at[h, 0], S_AO0 + h)
         wait_send(others(gu_zrecv.at[h], NZ), S_B0 + h)
         wait_send(others(hc.at[h, 0], NZ), S_C0 + h)
         wait_send(y_recv.at[h], S_D0 + h)
@@ -393,12 +406,18 @@
     wait_send(wd.at[0], S_WD)
     wait_send(hc.at[0, 0], S_CP)
     wait_send(others(gy_recv, ROWS), S_E)
-    wait_send(gy_give, S_EP)
+    wait_send(gy_mat.at[0], S_EP)
     wait_send(others(gh_zrecv, NZ), S_F)
-    wait_send(others(ac.at[0], NZ), S_G)
-    wait_send(ac.at[0], S_GP)
+    wait_send(others(ghc.at[0], NZ), S_G)
+    wait_send(others(fc.at[0], NZ), S_FC)
+    wait_send(wg.at[0], S_WG)
+    wait_send(wu.at[0], S_WU)
+    wait_send(x_full.at[0], S_X)
+    wait_send(act_mat.at[0, 0], S_AG)
+    wait_send(act_mat.at[1, 0], S_AU)
     wait_send(y_give, S_Y)
-    wait_send(gt_recv, S_H)
+    wait_send(others(gt_recv.at[0], ROWS), S_H)
+    wait_send(gt_recv.at[0], S_HO)
     for store in stores:
         store.wait()
 
@@ -438,19 +457,16 @@
             pltpu.SMEM(buckets.shape, jnp.int32),
             pltpu.VMEM(tokens.shape, BF16),
             pltpu.VMEM(target_table.shape, BF16),
-            pltpu.VMEM(w_gate.shape, BF16),
-            pltpu.VMEM(w_up.shape, BF16),
+            pltpu.VMEM((2, *w_gate.shape), BF16),
+            pltpu.VMEM((2, *w_up.shape), BF16),
             pltpu.VMEM((2, *w_down.shape), BF16),
-            pltpu.VMEM((2, 16, LANES), BF16),
-            pltpu.VMEM((2, ROWS, 16, LANES), BF16),
+            pltpu.VMEM((2, 2, 8, LANES), BF16),
+            pltpu.VMEM((2, 2, ROWS, 8, LANES), BF16),
             pltpu.VMEM((ROWS * 16, LANES), F32),
-            pltpu.VMEM((2, TOK, wide), BF16),
-            pltpu.VMEM((2, NZ, 16, width), F32),
+            pltpu.VMEM((2, 2, TOK // 2, wide), BF16),
+            pltpu.VMEM((2, TOK // 2, wide), BF16),
             pltpu.VMEM((2, NZ, 16, width), BF16),
             pltpu.VMEM((2, NZ, 16, width), BF16),
-            pltpu.VMEM((2, NZ, 16, width), BF16),
-            pltpu.VMEM((2, NZ, 16, width), BF16),
-            pltpu.VMEM((16, width), F32),
             pltpu.VMEM((2, 2, NZ, 16, half_width), BF16),
             pltpu.VMEM((2, TOK // 2, width), BF16),
             pltpu.VMEM((ROWS * 16, LANES), F32),
@@ -464,20 +480,20 @@
             pltpu.VMEM((16, LANES), BF16),
             pltpu.VMEM((ROWS, 16, LANES), BF16),
             pltpu.VMEM((2, TOK // 2, wide), BF16),
-            pltpu.VMEM((TOK // 2, wide), BF16),
+            pltpu.VMEM((2, TOK // 2, wide), BF16),
             pltpu.VMEM((NZ, 16, half_width), BF16),
             pltpu.VMEM((NZ, 16, half_width), BF16),
             pltpu.VMEM((2, NZ, 16, width), BF16),
-            pltpu.VMEM((2, TOK, width), BF16),
-            pltpu.VMEM((ROWS, 16, LANES), BF16),
-            pltpu.VMEM((ROWS - 1, 16, LANES), BF16),
+            pltpu.VMEM((2, TOK // 2, width), F32),
+            pltpu.VMEM((2, NZ, 16, half_width), BF16),
+            pltpu.VMEM((2, 2, TOK // 2, width), BF16),
+            pltpu.VMEM((2, ROWS, 8, LANES), BF16),
+            pltpu.VMEM((2, ROWS, 8, LANES), BF16),
             *(pltpu.VMEM(a.shape, BF16) for a in outs),
             pltpu.SemaphoreType.DMA((NUM_SEMS,)),
             pltpu.SemaphoreType.DMA((NUM_SEMS,)),
             pltpu.SemaphoreType.DMA((7,)),
             pltpu.SemaphoreType.DMA((5,)),
-            pltpu.SemaphoreType.DMA((2, NZ)),
-            pltpu.SemaphoreType.DMA((NZ - 1,)),
         ],
         compiler_params=pltpu.CompilerParams(
             collective_id=0, has_side_effects=True, vmem_limit_bytes=VMEM_BYTES

time: 73 us -> 70.8 us (0.970)
  Pallas kernels: 72.2 us -> 70 us
    pallas_call x1, Pallas kernels: 69.4 us -> 67.2 us  [on_device(): pl.pallas_call(kernel, out_shape=tuple((jax.ShapeDtypeStruct(a.shape, BF1...]
where the time goes in v3:
time: 70.8 us; the launch traced here: 70.6 us
  Pallas kernels  70 us (99%)
    pallas_call x1, Pallas kernels, on_device(): pl.pallas_call(kernel, out_shape=tuple((jax.ShapeDtypeStruct(a.shape, BF1...  67.2 us
    pallas_call x1, Pallas kernels, on_device(): pl.pallas_call(write_out, out_shape=tuple((jax.ShapeDtypeStruct(a.shape,...  2.79 us

profile of v3, /device:TPU:1, one launch (start us, length us, event | category | flops | bytes accessed | tf_op | source)
XLA Modules:
  0.0 70.6 jit_solution(14337265733322360977)
XLA Ops:
  0.6 67.2 %swiglu_step.1 = (bf16[8,512]{1,0:T(8,128)(2,1)}, bf16[8,512]{1,0:T(8,128)(2,1)}, bf16[512,768]{1,0:T(8,128)(2,1)}, bf16[512,768]{1,0:T(8,128)(2,1)}, bf16[768,512]{1,0:T(8,128)(2,1)}) custom-call(s32[4]{0:T(128)} %rows_hbm.1, s32[4]{0:T(128)} %buckets_hbm.1, bf16[8,512]{1,0:T(8,128)(2,1)} %tokens_hbm.1, bf16[512,768]{1,0:T(8,128)(2,1)} %wg_hbm.1, ...), custom_call_target="tpu_custom_call" | custom-call | tf_op jit(solution)/shard_map/swiglu_step/pallas_call | solution.py:450
  67.8 2.8 %write_out.1 = (bf16[8,512]{1,0:T(8,128)(2,1)}, bf16[8,512]{1,0:T(8,128)(2,1)}, bf16[512,768]{1,0:T(8,128)(2,1)}, bf16[512,768]{1,0:T(8,128)(2,1)}, bf16[768,512]{1,0:T(8,128)(2,1)}) custom-call(bf16[8,512]{1,0:T(8,128)(2,1)} %get-tuple-element.10.refs_0_, bf16[8,512]{1,0:T(8,128)(2,1)} %get-tuple-element.11.refs_1_, ...), custom_call_target="tpu_custom_call" | custom-call | tf_op jit(solution)/shard_map/write_out/pallas_call | solution.py:503

commit v4 on v3

--- a/solution.py
+++ b/solution.py
@@ -215,10 +215,14 @@
     def tokens_spread(h):
         def one(m, carry):
             remote(xs.at[h, 1 - k], xr.at[h, k, m], S_AO0 + h, row_peer(m, 1, 1 - k))
+            return carry
+
+        def two(m, carry):
             remote(xs.at[h, k], xr.at[h, k, m], S_A0 + h, row_peer(m, 1))
             return carry
 
         lax.fori_loop(0, ROWS - 1, one, 0)
+        lax.fori_loop(0, ROWS - 1, two, 0)
         remote(xs.at[h, 1 - k], xr.at[h, k, ROWS - 1], S_AO0 + h, partner)
 
     def tokens_wait(h):
@@ -344,10 +348,14 @@
 
     def grad_out(m, carry):
         remote(gt_send.at[1 - k, m], gt_recv.at[k, m], S_HO, row_peer(m, -1, 1 - k))
+        return carry
+
+    def grad_own(m, carry):
         remote(gt_send.at[k, m], gt_recv.at[k, m], S_H, row_peer(m, -1))
         return carry
 
     lax.fori_loop(0, ROWS - 1, grad_out, 0)
+    lax.fori_loop(0, ROWS - 1, grad_own, 0)
     remote(gt_send.at[1 - k, ROWS - 1], gt_recv.at[k, ROWS - 1], S_HO, partner)
     remote(act_mat.at[0, k], act_mat.at[0, k], S_AG, partner)
     remote(act_mat.at[1, k], act_mat.at[1, k], S_AU, partner)

time: 70.8 us -> 70.4 us (level)
  no operation moved by 1% of the time
where the time goes in v4:
time: 70.4 us; the launch traced here: 70.2 us
  Pallas kernels  69.6 us (99%)
    pallas_call x1, Pallas kernels, on_device(): pl.pallas_call(kernel, out_shape=tuple((jax.ShapeDtypeStruct(a.shape, BF1...  66.8 us
    pallas_call x1, Pallas kernels, on_device(): pl.pallas_call(write_out, out_shape=tuple((jax.ShapeDtypeStruct(a.shape,...  2.79 us

profile of v4, /device:TPU:1, one launch (start us, length us, event | category | flops | bytes accessed | tf_op | source)
XLA Modules:
  0.0 70.2 jit_solution(4865966392704928484)
XLA Ops:
  0.6 66.8 %swiglu_step.1 = (bf16[8,512]{1,0:T(8,128)(2,1)}, bf16[8,512]{1,0:T(8,128)(2,1)}, bf16[512,768]{1,0:T(8,128)(2,1)}, bf16[512,768]{1,0:T(8,128)(2,1)}, bf16[768,512]{1,0:T(8,128)(2,1)}) custom-call(s32[4]{0:T(128)} %rows_hbm.1, s32[4]{0:T(128)} %buckets_hbm.1, bf16[8,512]{1,0:T(8,128)(2,1)} %tokens_hbm.1, bf16[512,768]{1,0:T(8,128)(2,1)} %wg_hbm.1, ...), custom_call_target="tpu_custom_call" | custom-call | tf_op jit(solution)/shard_map/swiglu_step/pallas_call | solution.py:458
  67.4 2.8 %write_out.1 = (bf16[8,512]{1,0:T(8,128)(2,1)}, bf16[8,512]{1,0:T(8,128)(2,1)}, bf16[512,768]{1,0:T(8,128)(2,1)}, bf16[512,768]{1,0:T(8,128)(2,1)}, bf16[768,512]{1,0:T(8,128)(2,1)}) custom-call(bf16[8,512]{1,0:T(8,128)(2,1)} %get-tuple-element.10.refs_0_, bf16[8,512]{1,0:T(8,128)(2,1)} %get-tuple-element.11.refs_1_, ...), custom_call_target="tpu_custom_call" | custom-call | tf_op jit(solution)/shard_map/write_out/pallas_call | solution.py:511
